TPU v7x, 256 devices: a whole 4x4x8 slice. The times are simulated.
256 devices in a mesh: gx: 32 (over z, y_hi, core), gy: 8 (over x, y_lo).
Axes of the slice: x: 4, y: 4 (y_hi: 2, y_lo: 2; y = y_hi * 2 + y_lo), z: 8, core: 2. Of those that a mesh axis runs over, the one named last changes fastest.
Arguments:
- positions: float32 [3, 65536], P(None, ('gx', 'gy')), may hold values from 0.3 to 63.7, as said below
- species: int32 [65536], P(('gx', 'gy')), may hold values from 0 to 9
- face_rows: int32 [4, 32768], P(None, ('gx', 'gy')), may hold values from 0 to 255, as said below
- corner_rows: int32 [4, 16384], P(None, ('gx', 'gy')), may hold values from 0 to 255, as said below
- pair_recv: int32 [13312, 128], P(('gx', 'gy')), may hold values from 0 to 255, as said below
- pair_send: int32 [13312, 128], P(('gx', 'gy')), may hold values from 0 to 1023, as said below
- block_count: int32 [256], P(('gx', 'gy')), may hold values from 0 to 52, as said below
- embedding: float32 [10, 128], replicated, may hold values from -6 to 6
- radial_in: float32 [2, 8, 64], replicated, may hold values from -2 to 2
- radial_mid: float32 [2, 64, 64], replicated, may hold values from -0.75 to 0.75
- radial_out: float32 [2, 64, 384], replicated, may hold values from -0.75 to 0.75
- self_weight: float32 [2, 128, 128], replicated, may hold values from -0.5 to 0.5
- product_weight: float32 [2, 512, 128], replicated, may hold values from -0.25 to 0.25
- readout_linear: float32 [128], replicated, may hold values from -0.5 to 0.5
- readout_hidden: float32 [128, 16], replicated, may hold values from -0.5 to 0.5
- readout_final: float32 [16], replicated, may hold values from -1.5 to 1.5
Outputs:
- forces: float32 [3, 65536], P(None, ('gx', 'gy'))
- atom_energy: float32 [65536], P(('gx', 'gy'))
Inputs may be any that keep to these rules, and one draw needn't show every extreme that they name: `positions`: x and y lie inside 0 to 2, z inside 0 to 64; the two atoms of any pair are more than 0.5 apart. `face_rows`: local indices of the domain's own atoms, distinct within a row. `corner_rows`: local indices of the domain's own atoms, distinct within a row. `pair_recv`: local indices of the domain's own atoms. `pair_send`: indices into the domain's extended list of 1024 atoms, never the receiver itself. `block_count`: a multiple of 4; 52 on some domain in every draw.
All inputs are finite; a program needn't handle non-finite values.
Results may differ from a plain program's by a relative error of at most 0.0003.
Values sent between devices are 32-bit elements; how exact they have to be, the bound alone decides.
A program may use at most 128 MiB of HBM per device.

v0:
```python
from functools import partial

import jax
import jax.numpy as jnp
from jax import lax
from jax.sharding import PartitionSpec as P

GB = 4
LAT = 2


highest = lax.Precision.HIGHEST
inv_neigh = 0.25
cutoff = 2.5
sharpness = 2.0
root_three = 3.0**0.5
root_five = 5.0**0.5
root_fifteen = 15.0**0.5
face_steps = ((1, 0), (-1, 0), (0, 1), (0, -1))
corner_steps = ((1, 1), (1, -1), (-1, 1), (-1, -1))


def passed_along(array, axis, by):
    size = lax.axis_size(axis)
    return lax.ppermute(array, axis, [(i, (i + by) % size) for i in range(size)])


def harmonics(unit_vec):
    coord_x = unit_vec[0]
    coord_y = unit_vec[1]
    coord_z = unit_vec[2]
    return jnp.stack(
        [
            jnp.ones_like(coord_x),
            root_three * coord_x,
            root_three * coord_y,
            root_three * coord_z,
            root_fifteen * coord_x * coord_y,
            root_fifteen * coord_y * coord_z,
            0.5 * root_five * (3.0 * coord_z * coord_z - 1.0),
            root_fifteen * coord_x * coord_z,
            0.5 * root_fifteen * (coord_x * coord_x - coord_y * coord_y),
        ]
    )


def pair_messages(vectors, sender_feats, radial_in, radial_mid, radial_out):
    distance = jnp.sqrt(jnp.sum(vectors * vectors, axis=0))
    harmonic_vals = harmonics(vectors / distance[None, :])
    scaled_dist = distance / cutoff
    envelope = jnp.where(scaled_dist < 1.0, (1.0 - scaled_dist * scaled_dist) ** 2, 0.0)
    basis_count = radial_in.shape[0]
    centres = jnp.arange(basis_count, dtype=jnp.float32) * (cutoff / (basis_count - 1))
    radial_basis = (
        jnp.exp(-sharpness * (distance[None, :] - centres[:, None]) ** 2) * envelope[None, :]
    )
    hidden_one = jax.nn.silu(jnp.einsum("bp,bh->ph", radial_basis, radial_in, precision=highest))
    hidden_two = jax.nn.silu(jnp.dot(hidden_one, radial_mid, precision=highest))
    radial = jnp.dot(hidden_two, radial_out, precision=highest)
    pair_total = radial.shape[0]
    channels = sender_feats.shape[1]
    radial = radial.reshape(pair_total, 3, channels)
    expanded = jnp.concatenate(
        [
            radial[:, 0:1, :],
            jnp.broadcast_to(radial[:, 1:2, :], (pair_total, 3, channels)),
            jnp.broadcast_to(radial[:, 2:3, :], (pair_total, 5, channels)),
        ],
        axis=1,
    )
    return expanded * jnp.transpose(harmonic_vals)[:, :, None] * sender_feats[:, None, :]


def node_update(accum, previous, self_weight, product_weight):
    scalar_part = accum[..., 0, :]
    vector_norm = jnp.sum(accum[..., 1:4, :] * accum[..., 1:4, :], axis=-2)
    tensor_norm = jnp.sum(accum[..., 4:9, :] * accum[..., 4:9, :], axis=-2)
    invariants = jnp.concatenate(
        [scalar_part, vector_norm, tensor_norm, scalar_part * scalar_part], axis=-1
    )
    return jnp.dot(previous, self_weight, precision=highest) + jnp.dot(
        invariants, product_weight, precision=highest
    )


def atom_energies(first_feats, second_feats, readout_linear, readout_hidden, readout_final):
    hidden = jax.nn.silu(jnp.dot(second_feats, readout_hidden, precision=highest))
    return jnp.dot(first_feats, readout_linear, precision=highest) + jnp.dot(
        hidden, readout_final, precision=highest
    )


def take_rows(values, index, row_axis):
    return jnp.take(values, index, axis=row_axis)


def add_rows(total, index, piece, row_axis):
    if row_axis == 0:
        return total.at[index].add(piece)
    return total.at[:, index].add(piece)


def split_rows(values, row_counts, row_axis):
    pieces = []
    offset = 0
    for row_count in row_counts:
        pieces.append(lax.slice_in_dim(values, offset, offset + row_count, axis=row_axis))
        offset = offset + row_count
    return pieces


def along_x(values, steps):
    return passed_along(values, "gx", steps)


def along_y(values, steps):
    return passed_along(values, "gy", steps)


def ghost_offsets(face_count, corner_count):
    columns = []
    for step_x, step_y in face_steps:
        columns.append(
            jnp.broadcast_to(
                jnp.array([-step_x * LAT, -step_y * LAT, 0.0], dtype=jnp.float32)[:, None],
                (3, face_count),
            )
        )
    for step_x, step_y in corner_steps:
        columns.append(
            jnp.broadcast_to(
                jnp.array([-step_x * LAT, -step_y * LAT, 0.0], dtype=jnp.float32)[:, None],
                (3, corner_count),
            )
        )
    return jnp.concatenate(columns, axis=1)


def spread_ghosts(values, face_rows, corner_rows, row_axis):
    face_ghosts = [None, None, None, None]
    corner_ghosts = [None, None, None, None]
    for slot_index in range(4):
        step_x, step_y = face_steps[slot_index]
        outgoing = take_rows(values, face_rows[slot_index], row_axis)
        face_ghosts[slot_index] = (
            along_x(outgoing, step_x) if step_x != 0 else along_y(outgoing, step_y)
        )
    for slot_index in range(4):
        step_x, step_y = corner_steps[slot_index]
        outgoing = take_rows(values, corner_rows[slot_index], row_axis)
        corner_ghosts[slot_index] = along_y(along_x(outgoing, step_x), step_y)
    return jnp.concatenate(face_ghosts + corner_ghosts, axis=row_axis)


def collect_ghosts(owned, ghost_grads, face_rows, corner_rows, row_axis):
    face_count = face_rows.shape[1]
    corner_count = corner_rows.shape[1]
    pieces = split_rows(ghost_grads, (face_count,) * 4 + (corner_count,) * 4, row_axis)
    face_back = pieces[:4]
    corner_back = pieces[4:]
    for slot_index in range(4):
        step_x, step_y = face_steps[slot_index]
        piece = face_back[slot_index]
        returned = along_x(piece, -step_x) if step_x != 0 else along_y(piece, -step_y)
        owned = add_rows(owned, face_rows[slot_index], returned, row_axis)
    for slot_index in range(4):
        step_x, step_y = corner_steps[slot_index]
        returned = along_x(along_y(corner_back[slot_index], -step_y), -step_x)
        owned = add_rows(owned, corner_rows[slot_index], returned, row_axis)
    return owned


def group_pairs(pair_recv, pair_send, group_index):
    receivers = lax.dynamic_slice_in_dim(pair_recv, group_index * GB, GB, 0).reshape(-1)
    senders = lax.dynamic_slice_in_dim(pair_send, group_index * GB, GB, 0).reshape(-1)
    return (receivers, senders)


def forward_sum(
    pos_ext, feat_ext, pair_recv, pair_send, groups, radial_in, radial_mid, radial_out, atom_count
):
    width = 9 * feat_ext.shape[1]

    def forward_add_group(group_index, accum):
        receivers, senders = group_pairs(pair_recv, pair_send, group_index)
        vectors = jnp.take(pos_ext, senders, axis=1) - jnp.take(pos_ext, receivers, axis=1)
        messages = pair_messages(
            vectors, jnp.take(feat_ext, senders, axis=0), radial_in, radial_mid, radial_out
        )
        return accum.at[receivers].add(messages.reshape(messages.shape[0], width))

    total = lax.fori_loop(0, groups, forward_add_group, jnp.zeros((atom_count, width), jnp.float32))
    return total * inv_neigh


def backward_pairs(
    pos_ext,
    feat_ext,
    pair_recv,
    pair_send,
    groups,
    radial_in,
    radial_mid,
    radial_out,
    grad_accum,
    need_feats,
):
    channels = feat_ext.shape[1]

    def messages_of(vectors, sender_feats):
        return pair_messages(vectors, sender_feats, radial_in, radial_mid, radial_out)

    def backward_add_group(group_index, carry):
        grad_pos, grad_feat = carry
        receivers, senders = group_pairs(pair_recv, pair_send, group_index)
        vectors = jnp.take(pos_ext, senders, axis=1) - jnp.take(pos_ext, receivers, axis=1)
        sender_feats = jnp.take(feat_ext, senders, axis=0)
        cotangent = jnp.take(grad_accum, receivers, axis=0).reshape(-1, 9, channels)
        unused_out, pullback = jax.vjp(messages_of, vectors, sender_feats)
        grad_vectors, grad_senders = pullback(cotangent)
        grad_pos = grad_pos.at[:, senders].add(grad_vectors).at[:, receivers].add(-grad_vectors)
        if need_feats:
            grad_feat = grad_feat.at[senders].add(grad_senders)
        return (grad_pos, grad_feat)

    if need_feats:
        feat_start = jnp.zeros(feat_ext.shape, jnp.float32)
    else:
        feat_start = jnp.zeros((1, 1), jnp.float32)
    start = (jnp.zeros(pos_ext.shape, jnp.float32), feat_start)
    return lax.fori_loop(0, groups, backward_add_group, start)


def per_device(
    positions,
    species,
    face_rows,
    corner_rows,
    pair_recv,
    pair_send,
    block_count,
    embedding,
    radial_in,
    radial_mid,
    radial_out,
    self_weight,
    product_weight,
    readout_linear,
    readout_hidden,
    readout_final,
):
    atom_count = positions.shape[1]
    channels = embedding.shape[1]
    groups = block_count[0] // GB
    packed = jnp.concatenate([positions, species.astype(jnp.float32)[None, :]], axis=0)
    ghost_pack = spread_ghosts(packed, face_rows, corner_rows, 1)
    ghost_pos = ghost_pack[0:3] + ghost_offsets(face_rows.shape[1], corner_rows.shape[1])
    pos_ext = jnp.concatenate([positions, ghost_pos], axis=1)
    species_ext = jnp.concatenate([species, ghost_pack[3].astype(jnp.int32)])
    onehot = (
        species_ext[:, None] == jnp.arange(embedding.shape[0], dtype=jnp.int32)[None, :]
    ).astype(jnp.float32)
    zero_ext = jnp.dot(onehot, embedding, precision=highest)
    accum_one = forward_sum(
        pos_ext,
        zero_ext,
        pair_recv,
        pair_send,
        groups,
        radial_in[0],
        radial_mid[0],
        radial_out[0],
        atom_count,
    ).reshape(atom_count, 9, channels)
    node_one = partial(node_update, self_weight=self_weight[0], product_weight=product_weight[0])
    first_feats, pull_one = jax.vjp(node_one, accum_one, zero_ext[:atom_count])
    first_ghost = spread_ghosts(first_feats, face_rows, corner_rows, 0)
    first_ext = jnp.concatenate([first_feats, first_ghost], axis=0)
    accum_two = forward_sum(
        pos_ext,
        first_ext,
        pair_recv,
        pair_send,
        groups,
        radial_in[1],
        radial_mid[1],
        radial_out[1],
        atom_count,
    ).reshape(atom_count, 9, channels)
    node_two = partial(node_update, self_weight=self_weight[1], product_weight=product_weight[1])
    second_feats, pull_two = jax.vjp(node_two, accum_two, first_feats)
    energy_fn = partial(
        atom_energies,
        readout_linear=readout_linear,
        readout_hidden=readout_hidden,
        readout_final=readout_final,
    )
    energies, energy_pull = jax.vjp(energy_fn, first_feats, second_feats)
    grad_first, grad_second = energy_pull(jnp.ones_like(energies))
    grad_accum_two, grad_previous = pull_two(grad_second)
    grad_pos_two, grad_feat_ext = backward_pairs(
        pos_ext,
        first_ext,
        pair_recv,
        pair_send,
        groups,
        radial_in[1],
        radial_mid[1],
        radial_out[1],
        grad_accum_two.reshape(atom_count, -1) * inv_neigh,
        True,
    )
    grad_first = grad_first + grad_previous + grad_feat_ext[:atom_count]
    grad_first = collect_ghosts(grad_first, grad_feat_ext[atom_count:], face_rows, corner_rows, 0)
    grad_accum_one = pull_one(grad_first)[0]
    grad_pos_one, unused_feat = backward_pairs(
        pos_ext,
        zero_ext,
        pair_recv,
        pair_send,
        groups,
        radial_in[0],
        radial_mid[0],
        radial_out[0],
        grad_accum_one.reshape(atom_count, -1) * inv_neigh,
        False,
    )
    grad_pos = grad_pos_one + grad_pos_two
    owned = collect_ghosts(
        grad_pos[:, :atom_count], grad_pos[:, atom_count:], face_rows, corner_rows, 1
    )
    return (-owned, energies)


def solution(mesh):
    return jax.shard_map(
        per_device,
        mesh=mesh,
        in_specs=(
            P(None, ("gx", "gy")),
            P(("gx", "gy")),
            P(None, ("gx", "gy")),
            P(None, ("gx", "gy")),
            P(("gx", "gy"), None),
            P(("gx", "gy"), None),
            P(("gx", "gy")),
            P(),
            P(),
            P(),
            P(),
            P(),
            P(),
            P(),
            P(),
            P(),
        ),
        out_specs=(P(None, ("gx", "gy")), P(("gx", "gy"))),
        check_vma=False,
    )
```

profile of v0, /device:TPU:1, one launch (start us, length us, event | category | flops | bytes accessed | tf_op | source)
XLA Modules:
  0.0 2009.5 jit_solution(11099912255624908365)
XLA Ops:
  27.6 5.4 collective-permute-start.10
  52.3 131.4 %while.50 = (s32[]{:T(128)}, f32[256,1152]{1,0:T(8,128)S(1)}, s32[]{:T(128)}, s32[52,128]{1,0:T(8,128)}, s32[52,128]{1,0:T(8,128)}, /*index=5*/f32[3,1024]{0,1:T...) while((s32[]{:T(128)}, f32[256,1152]{1,0:T(8,128)S(1)}, ...), condition=%wide.region_3.8_spmd, body=%wide.region_0.7_spmd.sunk | while | flops 182635536 | bytes 25157660 | solution.py:192
  72.0 6.8 scatter_fusion
  98.2 6.8 scatter_fusion
  124.5 6.8 scatter_fusion
  150.7 6.8 scatter_fusion
  177.0 6.8 scatter_fusion
  194.4 211.9 %collective-permute-start.13 = (f32[128,128]{1,0:T(8,128)S(1)}, f32[128,128]{1,0:T(8,128)S(1)}, u32[]{:S(2)}, u32[]{:S(2)}) collective-permute-start(f32[128,128]{1,0:T(8,128)S(1)} %broadcast_select_fusion.8), channel_id=1, source_target_pairs={{0,248},{8,0},{16,8},{24,16},{32,24},{40,32},{48,40},{56,48},{64,5... | collective-permute-start | bytes 196616 | tf_op jit(solution)/shard_map/ppermute | solution.py:25
  407.5 6.0 collective-permute-start.20
  413.5 4.9 collective-permute-start.22
  430.9 132.8 %while.51 = (s32[]{:T(128)}, f32[256,1152]{1,0:T(8,128)S(1)}, s32[]{:T(128)}, s32[52,128]{1,0:T(8,128)}, s32[52,128]{1,0:T(8,128)}, /*index=5*/f32[3,1024]{0,1:T...) while((s32[]{:T(128)}, f32[256,1152]{1,0:T(8,128)S(1)}, ...), condition=%wide.region_9.16_spmd, body=%wide.region_6.15_spmd.sunk | while | flops 182635536 | bytes 24289176 | solution.py:192
  450.8 6.8 scatter_fusion.1
  477.3 6.8 scatter_fusion.1
  503.8 6.8 scatter_fusion.1
  530.4 6.8 scatter_fusion.1
  556.9 6.8 scatter_fusion.1
  569.1 248.3 %while.52 = (s32[]{:T(128)}, f32[3,1024]{0,1:T(8,128)}, f32[1024,128]{1,0:T(8,128)S(1)}, s32[]{:T(128)}, s32[52,128]{1,0:T(8,128)}, /*index=5*/f32[3,1024]{0,1:T...) while((s32[]{:T(128)}, f32[3,1024]{0,1:T(8,128)}, ...), condition=%wide.region_24.32_spmd, body=%wide.region_12.31_spmd.sunk | while | flops 366555648 | bytes 40508196 | solution.py:231
  605.1 4.9 scatter_fusion.2
  610.2 4.9 scatter_fusion.3
  709.3 4.9 scatter_fusion.3
  819.0 612.5 %collective-permute-start.24 = (f32[128,128]{1,0:T(8,128)S(1)}, f32[128,128]{1,0:T(8,128)S(1)}, u32[]{:S(2)}, u32[]{:S(2)}) collective-permute-start(f32[128,128]{1,0:T(8,128)S(1)} %get-tuple-element.973), channel_id=1, source_target_pairs={{0,248},{8,0},{16,8},{24,16},{32,24},{40,32},{48,40},{56,48},{64,5... | collective-permute-start | bytes 196616 | tf_op jit(solution)/shard_map/ppermute | solution.py:25
  1458.8 198.3 %while.53 = (s32[]{:T(128)}, f32[3,1024]{0,1:T(8,128)}, s32[]{:T(128)}, s32[52,128]{1,0:T(8,128)}, f32[3,1024]{0,1:T(8,128)}, /*index=5*/s32[52,128]{1,0:T(8,128...) while((s32[]{:T(128)}, f32[3,1024]{0,1:T(8,128)}, ...), condition=%wide.region_43.51_spmd, body=%wide.region_33.50_spmd.sunk | while | flops 364786176 | bytes 38206228 | solution.py:231
  1662.2 318.6 %collective-permute-start.36 = (f32[3,128]{0,1:T(8,128)S(1)}, f32[3,128]{0,1:T(8,128)S(1)}, u32[]{:S(2)}, u32[]{:S(2)}) collective-permute-start(f32[3,128]{0,1:T(8,128)S(1)} %get-tuple-element.962), channel_id=1, source_target_pairs={{0,248},{8,0},{16,8},{24,16},{32,24},{40,32},{48,40},{56,48},{64,5... | collective-permute-start | bytes 4616 | tf_op jit(solution)/shard_map/ppermute | solution.py:25
  1987.5 6.1 collective-permute-start.41
  (1789 shorter events, 750.3 us)
Async XLA Ops:
  3.8 32.3 %collective-permute-start = (f32[4,128]{0,1:T(8,128)S(1)}, f32[4,128]{0,1:T(8,128)S(1)}, u32[]{:S(2)}, u32[]{:S(2)}) collective-permute-start(f32[4,128]{0,1:T(8,128)S(1)} %select_bitcast_fusion.3), channel_id=1, source_target_pairs={{0,8},{8,16},{16,24},{24,32},{32,40},{40,48},{48,56},{56,64},{64,7... | collective-permute-start | bytes 6152 | tf_op jit(solution)/shard_map/ppermute | solution.py:25
  9.0 30.8 %collective-permute-start.1 = (f32[4,128]{0,1:T(8,128)S(1)}, f32[4,128]{0,1:T(8,128)S(1)}, u32[]{:S(2)}, u32[]{:S(2)}) collective-permute-start(f32[4,128]{0,1:T(8,128)S(1)} %select_bitcast_fusion.2), channel_id=1, source_target_pairs={{0,248},{8,0},{16,8},{24,16},{32,24},{40,32},{48,40},{56,48},{64,5... | collective-permute-start | bytes 6152 | tf_op jit(solution)/shard_map/ppermute | solution.py:25
  9.9 29.9 %collective-permute-start.2 = (f32[4,128]{0,1:T(8,128)S(1)}, f32[4,128]{0,1:T(8,128)S(1)}, u32[]{:S(2)}, u32[]{:S(2)}) collective-permute-start(f32[4,128]{0,1:T(8,128)S(1)} %select_bitcast_fusion.1), channel_id=1, source_target_pairs={{0,1},{1,2},{2,3},{3,4},{4,5},{5,6},{6,7},{7,0},{8,9},{9,10},{10,1... | collective-permute-start | bytes 6152 | tf_op jit(solution)/shard_map/ppermute | solution.py:25
  33.0 16.5 collective-permute-start.3
  194.2 213.3 %collective-permute-start.12 = (f32[128,128]{1,0:T(8,128)S(1)}, f32[128,128]{1,0:T(8,128)S(1)}, u32[]{:S(2)}, u32[]{:S(2)}) collective-permute-start(f32[128,128]{1,0:T(8,128)S(1)} %broadcast_select_fusion.9), channel_id=1, source_target_pairs={{0,8},{8,16},{16,24},{24,32},{32,40},{40,48},{48,56},{56,64},{64,7... | collective-permute-start | bytes 196616 | tf_op jit(solution)/shard_map/ppermute | solution.py:25
  194.4 219.1 %collective-permute-start.13 = (f32[128,128]{1,0:T(8,128)S(1)}, f32[128,128]{1,0:T(8,128)S(1)}, u32[]{:S(2)}, u32[]{:S(2)}) collective-permute-start(f32[128,128]{1,0:T(8,128)S(1)} %broadcast_select_fusion.8), channel_id=1, source_target_pairs={{0,248},{8,0},{16,8},{24,16},{32,24},{40,32},{48,40},{56,48},{64,5... | collective-permute-start | bytes 196616 | tf_op jit(solution)/shard_map/ppermute | solution.py:25
  406.4 19.5 collective-permute-start.14
  407.3 15.0 collective-permute-start.18
  407.5 14.8 collective-permute-start.20
  817.4 616.0 %collective-permute-start.28 = (f32[64,128]{1,0:T(8,128)S(1)}, f32[64,128]{1,0:T(8,128)S(1)}, u32[]{:S(2)}, u32[]{:S(2)}) collective-permute-start(f32[64,128]{1,0:T(8,128)S(1)} %get-tuple-element.969), channel_id=1, source_target_pairs={{0,7},{1,0},{2,1},{3,2},{4,3},{5,4},{6,5},{7,6},{8,15},{9,8},{10,9... | collective-permute-start | bytes 98312 | tf_op jit(solution)/shard_map/ppermute | solution.py:25
  817.5 616.0 %collective-permute-start.30 = (f32[64,128]{1,0:T(8,128)S(1)}, f32[64,128]{1,0:T(8,128)S(1)}, u32[]{:S(2)}, u32[]{:S(2)}) collective-permute-start(f32[64,128]{1,0:T(8,128)S(1)} %get-tuple-element.968), channel_id=1, source_target_pairs={{0,1},{1,2},{2,3},{3,4},{4,5},{5,6},{6,7},{7,0},{8,9},{9,10},{10,1... | collective-permute-start | bytes 98312 | tf_op jit(solution)/shard_map/ppermute | solution.py:25
  819.0 622.7 %collective-permute-start.24 = (f32[128,128]{1,0:T(8,128)S(1)}, f32[128,128]{1,0:T(8,128)S(1)}, u32[]{:S(2)}, u32[]{:S(2)}) collective-permute-start(f32[128,128]{1,0:T(8,128)S(1)} %get-tuple-element.973), channel_id=1, source_target_pairs={{0,248},{8,0},{16,8},{24,16},{32,24},{40,32},{48,40},{56,48},{64,5... | collective-permute-start | bytes 196616 | tf_op jit(solution)/shard_map/ppermute | solution.py:25
  1431.5 13.7 collective-permute-start.25
  1431.5 13.7 collective-permute-start.26
  1436.6 14.1 collective-permute-start.27
  1438.6 13.5 collective-permute-start.29
  1658.4 322.4 %collective-permute-start.40 = (f32[3,64]{0,1:T(8,128)S(1)}, f32[3,64]{0,1:T(8,128)S(1)}, u32[]{:S(2)}, u32[]{:S(2)}) collective-permute-start(f32[3,64]{0,1:T(8,128)S(1)} %get-tuple-element.958), channel_id=1, source_target_pairs={{0,7},{1,0},{2,1},{3,2},{4,3},{5,4},{6,5},{7,6},{8,15},{9,8},{10,9... | collective-permute-start | bytes 2312 | tf_op jit(solution)/shard_map/ppermute | solution.py:25
  1658.5 322.3 %collective-permute-start.42 = (f32[3,64]{0,1:T(8,128)S(1)}, f32[3,64]{0,1:T(8,128)S(1)}, u32[]{:S(2)}, u32[]{:S(2)}) collective-permute-start(f32[3,64]{0,1:T(8,128)S(1)} %get-tuple-element.957), channel_id=1, source_target_pairs={{0,1},{1,2},{2,3},{3,4},{4,5},{5,6},{6,7},{7,0},{8,9},{9,10},{10,1... | collective-permute-start | bytes 2312 | tf_op jit(solution)/shard_map/ppermute | solution.py:25
  1660.0 322.3 %collective-permute-start.44 = (f32[3,64]{0,1:T(8,128)S(1)}, f32[3,64]{0,1:T(8,128)S(1)}, u32[]{:S(2)}, u32[]{:S(2)}) collective-permute-start(f32[3,64]{0,1:T(8,128)S(1)} %get-tuple-element.956), channel_id=1, source_target_pairs={{0,7},{1,0},{2,1},{3,2},{4,3},{5,4},{6,5},{7,6},{8,15},{9,8},{10,9... | collective-permute-start | bytes 2312 | tf_op jit(solution)/shard_map/ppermute | solution.py:25
  1662.2 331.4 %collective-permute-start.36 = (f32[3,128]{0,1:T(8,128)S(1)}, f32[3,128]{0,1:T(8,128)S(1)}, u32[]{:S(2)}, u32[]{:S(2)}) collective-permute-start(f32[3,128]{0,1:T(8,128)S(1)} %get-tuple-element.962), channel_id=1, source_target_pairs={{0,248},{8,0},{16,8},{24,16},{32,24},{40,32},{48,40},{56,48},{64,5... | collective-permute-start | bytes 4616 | tf_op jit(solution)/shard_map/ppermute | solution.py:25
  1980.8 16.6 collective-permute-start.37
  1980.8 16.6 collective-permute-start.38
  1980.8 21.6 %collective-permute-start.39 = (f32[3,128]{0,1:T(8,128)S(1)}, f32[3,128]{0,1:T(8,128)S(1)}, u32[]{:S(2)}, u32[]{:S(2)}) collective-permute-start(f32[3,128]{0,1:T(8,128)S(1)} %get-tuple-element.959), channel_id=1, source_target_pairs={{0,1},{1,2},{2,3},{3,4},{4,5},{5,6},{6,7},{7,0},{8,9},{9,10},{10,1... | collective-permute-start | bytes 4616 | tf_op jit(solution)/shard_map/ppermute | solution.py:25
  1987.5 16.4 collective-permute-start.41
  (417 other events, 6924.6 us)
where the time goes:
time: 2040 us; the launch traced here: 2010 us
  starting transfers between devices  1220 us (60%)
  other arithmetic  371 us (18%)
  local copies, waits for them, and re-layouts  333 us (16%)
  matrix products  66.2 us (3%)
    ppermute x48, starting transfers between devices, passed_along(): lax.ppermute(array, axis, [(i, (i + by) % size) for i in range(size)])  1220 us
    scatter-add x20, other arithmetic, backward_add_group(): grad_pos.at[:, senders].add(grad_vectors).at[:, receivers]  96.9 us
    scatter-add x10, other arithmetic, forward_add_group(): return accum.at[receivers].add(messages.reshape(messages.shape[0], width))  67.6 us
  transfers between devices with their start and end apart: 48, of which 3 were waited for; matrix products, arithmetic and copies ran while one was open for 2% of the time, Pallas kernels for 0%

commit v1 on v0

v1 whole, which is shorter than its diff:
```python
from functools import partial

import jax
import jax.numpy as jnp
from jax import lax
from jax.experimental import pallas as pl
from jax.experimental.pallas import tpu as pltpu
from jax.sharding import PartitionSpec as P

f32 = jnp.float32
bf16 = jnp.bfloat16
i32 = jnp.int32

LAT = 2
C = 128
RH = 64
NB = 8
ATOMS = 256
EXT = 1024
NBLK = 52
PB = 128
PAIRS = NBLK * PB
TM = 512
T = 256
SUB = 128
ROWS = 56
STEPS = ((1, 0), (-1, 0), (0, 1), (0, -1), (1, 1), (1, -1), (-1, 1), (-1, -1))
CUTOFF = 2.5
SHARP = 2.0
Q3 = 3.0**0.5
Q5 = 5.0**0.5
Q15 = 15.0**0.5
INV_NEIGH = 0.25
HIGH = lax.Precision.HIGHEST
MESH = pl.DeviceIdType.MESH
L_OF_M = (0, 1, 1, 1, 2, 2, 2, 2, 2)


def dot(a, b):
    return lax.dot_general(a, b, (((1,), (0,)), ((), ())), preferred_element_type=f32)


def dot_nt(a, b):
    return lax.dot_general(a, b, (((1,), (1,)), ((), ())), preferred_element_type=f32)


def dot_exact(a, b):
    return lax.dot_general(
        a, b, (((1,), (0,)), ((), ())), precision=HIGH, preferred_element_type=f32
    )


def parts2(x):
    hi = x.astype(bf16).astype(f32)
    return hi, (x - hi).astype(bf16).astype(f32)


def parts3(x):
    hi = x.astype(bf16).astype(f32)
    rest = x - hi
    mid = rest.astype(bf16).astype(f32)
    return hi, mid, (rest - mid).astype(bf16).astype(f32)


def split2(x):
    hi = x.astype(bf16)
    return hi, (x - hi.astype(f32)).astype(bf16)


def activations(x):
    hi, lo = split2(x)
    return jnp.concatenate([hi, lo, hi, lo], axis=0)


def weights(w):
    hi, lo = parts2(w)
    return jnp.concatenate([hi, hi, lo, lo], axis=0).T.astype(bf16)


def slot_of(k):
    return (128 * k, 128) if k < 4 else (512 + 64 * (k - 4), 64)


def tile_of(k):
    return k if k < 4 else 4 + (k - 4) // 2


def kernel_body(
    sizes,
    pos,
    species,
    face_rows,
    corner_rows,
    pair_recv,
    pair_send,
    block_count,
    embedding,
    radial_in,
    radial_mid,
    radial_out,
    self_weight,
    product_weight,
    readout_linear,
    readout_hidden,
    readout_final,
    forces,
    energies,
    *scratch,
):
    (
        rows6,
        oh6,
        oh6t,
        psrc,
        posout,
        posin,
        ptab,
        geop,
        georow,
        sendrow,
        recvm,
        ohs,
        ohr,
        emb3,
        win4,
        wmid4,
        wout4,
        bmid4,
        bin4,
        bout2,
        bout1,
        z1s,
        z2s,
        rs,
        fg,
        msg,
        acc,
        acc1,
        acc2,
        gacc,
        gbuf,
        gf,
        gr,
        ge,
        f0t,
        f1t,
        fsend,
        fghost,
        fext,
        gfirst,
        gsend,
        gret,
        gv,
        fs,
        fr,
        gpout,
        gpin,
        send_sem,
        recv_sem,
    ) = scratch
    sums = (acc1, acc2)
    nx, ny = sizes
    alone = nx * ny == 1
    mx = lax.axis_index("gx")
    my = lax.axis_index("gy")

    def neighbour(k, sign):
        dx, dy = STEPS[k]
        return (lax.rem(mx + sign * dx + nx, nx), lax.rem(my + sign * dy + ny, ny))

    if not alone:
        barrier = pltpu.get_barrier_semaphore()
        for k in range(8):
            pl.semaphore_signal(barrier, inc=1, device_id=neighbour(k, 1), device_id_type=MESH)

    def copies(phase, source, target, sign):
        made = []
        for k in range(8):
            if alone:
                made.append(
                    pltpu.make_async_copy(source(k), target(k), recv_sem.at[phase * 8 + k])
                )
            else:
                made.append(
                    pltpu.make_async_remote_copy(
                        src_ref=source(k),
                        dst_ref=target(k),
                        send_sem=send_sem.at[phase * 8 + k],
                        recv_sem=recv_sem.at[phase * 8 + k],
                        device_id=neighbour(k, sign),
                        device_id_type=MESH,
                    )
                )
        return made

    def start(made):
        for c in made:
            c.start()

    def finish(made):
        for c in made:
            c.wait()

    rows6[...] = jnp.zeros_like(rows6)
    rows6[0:4, :] = face_rows[...]
    rows6[4:5, :] = jnp.concatenate([corner_rows[0:1, :], corner_rows[1:2, :]], axis=1)
    rows6[5:6, :] = jnp.concatenate([corner_rows[2:3, :], corner_rows[3:4, :]], axis=1)
    rows_t = rows6[...].astype(f32).T
    atom_sub = lax.broadcasted_iota(i32, (ATOMS, 128), 0)
    atom_lane = lax.broadcasted_iota(i32, (128, ATOMS), 1)
    for h in range(6):
        oh6[:, h * 128 : (h + 1) * 128] = (atom_sub == rows6[h : h + 1, :]).astype(bf16)
        col = jnp.broadcast_to(rows_t[:, h : h + 1], (128, ATOMS)).astype(i32)
        oh6t[h * 128 : (h + 1) * 128, :] = (atom_lane == col).astype(bf16)

    psrc[...] = jnp.zeros_like(psrc)
    psrc[0:3, :] = pos[...]
    psrc[3:4, :] = species[...].astype(f32)
    own = psrc[...]
    three = jnp.concatenate(parts3(own), axis=0).astype(bf16)
    lent = dot(three, oh6[...])
    lent = lent[0:8] + lent[8:16] + lent[16:24]
    for h in range(6):
        posout[h] = lent[:, h * 128 : (h + 1) * 128]
    if not alone:
        pl.semaphore_wait(barrier, 8)
    sent = copies(0, lambda k: posout.at[tile_of(k)], lambda k: posin.at[k], 1)
    start(sent)

    ext_sub = lax.broadcasted_iota(i32, (EXT, PB), 0)
    live = lax.broadcasted_iota(i32, (NBLK, PB), 0) < block_count[0]
    recvm[...] = jnp.where(live, pair_recv[...], -1)

    def build(b, carry):
        cols = pl.ds(pl.multiple_of(b * PB, PB), PB)
        send = pair_send[pl.ds(b, 1), :]
        ohs[:, cols] = (ext_sub == send).astype(bf16)
        ohr[:, cols] = (atom_sub == recvm[pl.ds(b, 1), :]).astype(bf16)
        sendrow[0:1, cols] = send
        return carry

    lax.fori_loop(0, NBLK, build, 0)

    emb = embedding[...]
    padding = jnp.zeros((6, C), f32)
    pieces = []
    for piece in parts3(emb):
        pieces += [piece, padding]
    pieces.append(jnp.zeros((80, C), f32))
    emb3[...] = jnp.concatenate(pieces, axis=0).T.astype(bf16)

    def prepare(t):
        win = radial_in[t]
        wmid = radial_mid[t]
        wout = radial_out[t]
        win4[...] = weights(win)
        wmid4[...] = weights(wmid)
        wout4[...] = weights(wout)

    def prepare_back(t):
        win = radial_in[t]
        wmid = radial_mid[t]
        wout = radial_out[t]
        bmid4[...] = weights(wmid.T)
        bin4[...] = jnp.concatenate([weights(win.T), jnp.zeros((8, 4 * RH), bf16)], axis=0)
        hi, lo = split2(wout)
        bout2[0:RH, :] = hi
        bout2[RH : 2 * RH, :] = lo
        bout1[...] = hi

    prepare(0)
    species16 = lax.broadcasted_iota(i32, (128, T), 0) & 15
    f0t[...] = dot(emb3[...], (species16 == species[...]).astype(bf16))

    finish(sent)

    low_half = lax.broadcasted_iota(i32, (8, 128), 1) < 64
    tiles = [own[:, 0:128], own[:, 128:256]]
    shifted = []
    for k in range(8):
        dx, dy = STEPS[k]
        got = posin[k]
        sub = lax.broadcasted_iota(i32, (8, 128), 0)
        shift = jnp.where(sub == 0, f32(dx * LAT), jnp.where(sub == 1, f32(dy * LAT), f32(0)))
        shifted.append(got - shift)
    tiles += shifted[0:4]
    tiles.append(jnp.where(low_half, shifted[4], shifted[5]))
    tiles.append(jnp.where(low_half, shifted[6], shifted[7]))
    for h in range(8):
        ptab[h] = tiles[h]

    send = pair_send[...]
    send_lo = send & 127
    send_hi = lax.shift_right_logical(send, 7)
    recv = pair_recv[...]
    recv_lo = recv & 127
    recv_hi = lax.shift_right_logical(recv, 7)

    def gather(c, lo, hi, count):
        total = jnp.zeros((NBLK, PB), f32)
        for h in range(count):
            row = jnp.broadcast_to(ptab[h][c : c + 1, :], (NBLK, PB))
            total = jnp.where(hi == h, jnp.take_along_axis(row, lo, axis=1), total)
        return total

    vec = [gather(c, send_lo, send_hi, 8) - gather(c, recv_lo, recv_hi, 2) for c in range(3)]
    sender_species = gather(3, send_lo, send_hi, 8)
    square = vec[0] * vec[0] + vec[1] * vec[1] + vec[2] * vec[2]
    square = jnp.where(live, square, 1.0)
    dist = jnp.sqrt(square)
    inv = 1.0 / dist
    ux, uy, uz = [v / dist for v in vec]
    scaled = dist * (1.0 / CUTOFF)
    inside = scaled < 1.0
    room = 1.0 - scaled * scaled
    env = jnp.where(inside, room * room, 0.0)
    denv = jnp.where(inside, (-4.0 / CUTOFF) * scaled * room, 0.0)
    values = [
        dist,
        ux,
        uy,
        uz,
        inv,
        env,
        denv,
        sender_species,
        Q3 * ux,
        Q3 * uy,
        Q3 * uz,
        Q15 * ux * uy,
        Q15 * uy * uz,
        0.5 * Q5 * (3.0 * uz * uz - 1.0),
        Q15 * ux * uz,
        0.5 * Q15 * (ux * ux - uy * uy),
    ]
    for n in range(16):
        geop[n * ROWS : n * ROWS + NBLK, :] = values[n]
    for b in range(NBLK):
        georow[:, b * PB : (b + 1) * PB] = geop[pl.ds(b, 16, stride=ROWS), :]

    def basis_of(geo, width):
        dist = geo[0:1]
        centre = lax.broadcasted_iota(i32, (NB, width), 0).astype(f32) * (CUTOFF / (NB - 1))
        away = dist - centre
        return away, jnp.exp(-SHARP * away * away)

    def radial_pass(i, carry):
        cols = pl.ds(pl.multiple_of(i * TM, TM), TM)
        geo = georow[:, cols]
        away, bump = basis_of(geo, TM)
        hi, lo = parts2(bump * geo[5:6])
        z1 = dot(win4[...], jnp.concatenate([hi, lo, hi, lo], axis=0).astype(bf16))
        z1s[:, cols] = z1
        z2 = dot(wmid4[...], activations(z1 * jax.nn.sigmoid(z1)))
        z2s[:, cols] = z2
        rs[:, cols] = dot(wout4[...], activations(z2 * jax.nn.sigmoid(z2)))
        return carry

    def radial_all():
        lax.fori_loop(0, PAIRS // TM, radial_pass, 0)

    def first_senders(cols):
        return dot(emb3[...], (species16 == georow[7:8, cols].astype(i32)).astype(bf16))

    def second_senders(cols):
        both = dot(fext[...], ohs[:, cols])
        return both[0:C] + both[C : 2 * C]

    def forward(t, senders):
        acc[...] = jnp.zeros_like(acc)

        def step(i, carry):
            base = pl.multiple_of(i * T, T)
            cols = pl.ds(base, T)
            fg[:, cols] = senders(cols)
            for s in range(0, T, SUB):
                sub = pl.ds(pl.multiple_of(base + s, SUB), SUB)
                ys = [jnp.broadcast_to(georow[8 + m : 9 + m, sub], (16, SUB)) for m in range(8)]
                for c in range(0, C, 16):
                    f = fg[c : c + 16, sub]
                    p = [rs[l * C + c : l * C + c + 16, sub] * f for l in range(3)]
                    for m in range(9):
                        value = p[0] if m == 0 else p[L_OF_M[m]] * ys[m - 1]
                        hi, lo = split2(value)
                        msg[m * C + c : m * C + c + 16, s : s + SUB] = hi
                        msg[m * C + c : m * C + c + 16, T + s : T + s + SUB] = lo
            hot = ohr[:, cols]
            acc[...] += dot_nt(msg[...], jnp.concatenate([hot, hot], axis=1))
            return carry

        lax.fori_loop(0, PAIRS // T, step, 0)
        sums[t][...] = acc[...] * INV_NEIGH

    def invariants(t):
        accn = sums[t]
        a0 = accn[0:C]
        v = accn[C : 2 * C] ** 2
        for m in range(2, 4):
            v = v + accn[m * C : (m + 1) * C] ** 2
        w = accn[4 * C : 5 * C] ** 2
        for m in range(5, 9):
            w = w + accn[m * C : (m + 1) * C] ** 2
        return jnp.concatenate([a0, v, w, a0 * a0], axis=0)

    def node(t, previous):
        return dot_exact(self_weight[t].T, previous) + dot_exact(
            product_weight[t].T, invariants(t)
        )

    def node_back(t, grad):
        accn = sums[t]
        ginv = dot_exact(product_weight[t], grad) * INV_NEIGH
        for m in range(9):
            a = accn[m * C : (m + 1) * C]
            if m == 0:
                g = ginv[0:C] + 2.0 * a * ginv[3 * C : 4 * C]
            else:
                l = L_OF_M[m]
                g = 2.0 * a * ginv[l * C : (l + 1) * C]
            hi, lo = split2(g)
            gacc[m * C : (m + 1) * C, 0:ATOMS] = hi
            gacc[m * C : (m + 1) * C, ATOMS : 2 * ATOMS] = lo

    def backward(first):
        def step(i, carry):
            base = pl.multiple_of(i * T, T)
            cols = pl.ds(base, T)
            hot = ohr[:, cols]
            gbuf[...] = dot(gacc[...], jnp.concatenate([hot, hot], axis=0))
            gys = []
            for s in range(0, T, SUB):
                sub = pl.ds(pl.multiple_of(base + s, SUB), SUB)
                ys = [jnp.broadcast_to(georow[8 + m : 9 + m, sub], (16, SUB)) for m in range(8)]
                dy = [jnp.zeros((16, SUB), f32) for m in range(8)]
                for c in range(0, C, 16):
                    f = fg[c : c + 16, sub]
                    r = [rs[l * C + c : l * C + c + 16, sub] for l in range(3)]
                    p = [x * f for x in r]
                    tot = [None, None, None]
                    for m in range(9):
                        g = gbuf[m * C + c : m * C + c + 16, s : s + SUB]
                        l = L_OF_M[m]
                        term = g if m == 0 else g * ys[m - 1]
                        tot[l] = term if tot[l] is None else tot[l] + term
                        if m > 0:
                            dy[m - 1] = dy[m - 1] + p[l] * g
                    if not first:
                        gfv = r[0] * tot[0] + r[1] * tot[1] + r[2] * tot[2]
                        hi, lo = split2(gfv)
                        gf[c : c + 16, s : s + SUB] = hi
                        gf[C + c : C + c + 16, s : s + SUB] = lo
                    for l in range(3):
                        hi, lo = split2(tot[l] * f)
                        gr[l * C + c : l * C + c + 16, s : s + SUB] = hi
                        gr[l * C + c : l * C + c + 16, T + s : T + s + SUB] = lo
                gys.append([jnp.sum(x, axis=0, keepdims=True) for x in dy])
            gy = [jnp.concatenate([part[m] for part in gys], axis=1) for m in range(8)]
            if not first:
                ge[...] += dot_nt(ohs[:, cols], gf[...])
            both = dot(bout2[...], gr[:, 0:T])
            gh2 = both[0:RH] + both[RH : 2 * RH] + dot(bout1[...], gr[:, T : 2 * T])
            z2 = z2s[:, cols]
            sg = jax.nn.sigmoid(z2)
            gh1 = dot(bmid4[...], activations(gh2 * (sg * (1.0 + z2 * (1.0 - sg)))))
            z1 = z1s[:, cols]
            sg = jax.nn.sigmoid(z1)
            gb = dot(bin4[...], activations(gh1 * (sg * (1.0 + z1 * (1.0 - sg)))))[0:NB]
            geo = georow[:, cols]
            away, bump = basis_of(geo, T)
            slope = bump * (geo[6:7] - (2.0 * SHARP) * away * geo[5:6])
            gdist = jnp.sum(gb * slope, axis=0, keepdims=True)
            ux, uy, uz = geo[1:2], geo[2:3], geo[3:4]
            gux = Q3 * gy[0] + Q15 * (uy * gy[3] + uz * gy[6] + ux * gy[7])
            guy = Q3 * gy[1] + Q15 * (ux * gy[3] + uz * gy[4] - uy * gy[7])
            guz = Q3 * gy[2] + Q15 * (uy * gy[4] + ux * gy[6]) + (3.0 * Q5) * uz * gy[5]
            along = gux * ux + guy * uy + guz * uz
            inv = geo[4:5]
            pull = gdist - inv * along
            out = [pull * ux + inv * gux, pull * uy + inv * guy, pull * uz + inv * guz]
            if not first:
                for n in range(3):
                    gv[n : n + 1, cols] = out[n]
            else:
                out = [out[n] + gv[n : n + 1, cols] for n in range(3)]
                cut = [parts2(x) for x in out]
                zero = jnp.zeros((2, T), f32)
                base8 = jnp.concatenate([x[0] for x in cut] + [x[1] for x in cut] + [zero], axis=0)
                idx = sendrow[0:1, cols]
                high = lax.shift_right_logical(idx, 7)
                lhs = jnp.concatenate(
                    [jnp.where(high == h, base8, 0.0) for h in range(8)], axis=0
                ).astype(bf16)
                low = (lax.broadcasted_iota(i32, (128, T), 0) == (idx & 127)).astype(bf16)
                fs[...] += dot_nt(lhs, low)
                lhs = jnp.concatenate([base8, jnp.zeros((8, T), f32)], axis=0).astype(bf16)
                fr[...] += dot_nt(lhs, hot)
            return carry

        lax.fori_loop(0, PAIRS // T, step, 0)

    radial_all()
    forward(0, first_senders)
    f1t[...] = node(0, f0t[...])

    feat = f1t[...]
    rows = feat.T
    gathered = dot(oh6t[...], jnp.concatenate(parts3(rows), axis=1).astype(bf16))
    fsend[...] = gathered[:, 0:C] + gathered[:, C : 2 * C] + gathered[:, 2 * C : 3 * C]
    sent = copies(
        1, lambda k: fsend.at[pl.ds(*slot_of(k))], lambda k: fghost.at[pl.ds(*slot_of(k))], 1
    )
    start(sent)
    gsend[0:ATOMS, :] = jnp.zeros((ATOMS, C), f32)
    prepare(1)
    prepare_back(1)
    radial_all()
    finish(sent)
    hi, lo = split2(feat)
    fext[0:C, 0:ATOMS] = hi
    fext[C : 2 * C, 0:ATOMS] = lo
    hi, lo = split2(fghost[...].T)
    fext[0:C, ATOMS:EXT] = hi
    fext[C : 2 * C, ATOMS:EXT] = lo

    forward(1, second_senders)
    second = node(1, feat)
    hidden = dot_exact(readout_hidden[...].T, second)
    sg = jax.nn.sigmoid(hidden)
    energies[...] = dot_exact(readout_linear[...], feat) + dot_exact(
        readout_final[...], hidden * sg
    )
    weight = readout_final[...].T
    ghidden = weight * (sg * (1.0 + hidden * (1.0 - sg)))
    gsecond = dot_exact(readout_hidden[...], ghidden)
    gfirst[...] = readout_linear[...].T + dot_exact(self_weight[1], gsecond)
    node_back(1, gsecond)
    ge[...] = jnp.zeros_like(ge)
    backward(False)

    gsend[...] = ge[:, 0:C] + ge[:, C : 2 * C]

    def ghost(k):
        offset, size = slot_of(k)
        return gsend.at[pl.ds(ATOMS + offset, size)]

    sent = copies(2, ghost, lambda k: gret.at[pl.ds(*slot_of(k))], -1)
    start(sent)
    prepare(0)
    prepare_back(0)
    radial_all()

    def senders_pass(i, carry):
        cols = pl.ds(pl.multiple_of(i * T, T), T)
        fg[:, cols] = first_senders(cols)
        return carry

    lax.fori_loop(0, PAIRS // T, senders_pass, 0)
    fs[...] = jnp.zeros_like(fs)
    fr[...] = jnp.zeros_like(fr)
    finish(sent)
    returned = dot(oh6[...], jnp.concatenate(parts3(gret[...]), axis=1).astype(bf16))
    mine = gsend[0:ATOMS, :] + returned[:, 0:C] + returned[:, C : 2 * C] + returned[:, 2 * C :]
    node_back(0, gfirst[...] + mine.T)
    backward(True)

    nothing = jnp.zeros((5, 128), f32)
    tiles = []
    for h in range(8):
        part = fs[8 * h : 8 * h + 8, :]
        tiles.append(jnp.concatenate([part[0:3] + part[3:6], nothing], axis=0))
    for h in range(6):
        gpout[h] = tiles[h + 2]
    sent = copies(3, lambda k: gpout.at[tile_of(k)], lambda k: gpin.at[k], -1)
    start(sent)
    own = jnp.concatenate(tiles[0:2], axis=1)[0:3] - (fr[0:3, :] + fr[3:6, :])
    finish(sent)
    back = [gpin[k] for k in range(4)]
    back.append(jnp.where(low_half, gpin[4], gpin[5]))
    back.append(jnp.where(low_half, gpin[6], gpin[7]))
    three = jnp.concatenate(parts3(jnp.concatenate(back, axis=1)), axis=0).astype(bf16)
    added = dot_nt(three, oh6[...])
    forces[...] = -(own + added[0:3] + added[8:11] + added[16:19])


SCRATCH = (
    ((8, 128), i32),
    ((ATOMS, 768), bf16),
    ((768, ATOMS), bf16),
    ((8, ATOMS), f32),
    ((6, 8, 128), f32),
    ((8, 8, 128), f32),
    ((8, 8, 128), f32),
    ((16 * ROWS, 128), f32),
    ((16, PAIRS), f32),
    ((8, PAIRS), i32),
    ((NBLK, PB), i32),
    ((EXT, PAIRS), bf16),
    ((ATOMS, PAIRS), bf16),
    ((C, 128), bf16),
    ((RH, 4 * NB), bf16),
    ((RH, 4 * RH), bf16),
    ((3 * C, 4 * RH), bf16),
    ((RH, 4 * RH), bf16),
    ((2 * NB, 4 * RH), bf16),
    ((2 * RH, 3 * C), bf16),
    ((RH, 3 * C), bf16),
    ((RH, PAIRS), f32),
    ((RH, PAIRS), f32),
    ((3 * C, PAIRS), f32),
    ((C, PAIRS), f32),
    ((9 * C, 2 * T), bf16),
    ((9 * C, ATOMS), f32),
    ((9 * C, ATOMS), f32),
    ((9 * C, ATOMS), f32),
    ((9 * C, 2 * ATOMS), bf16),
    ((9 * C, T), f32),
    ((2 * C, T), bf16),
    ((3 * C, 2 * T), bf16),
    ((EXT, 2 * C), f32),
    ((C, ATOMS), f32),
    ((C, ATOMS), f32),
    ((768, C), f32),
    ((768, C), f32),
    ((2 * C, EXT), bf16),
    ((C, ATOMS), f32),
    ((EXT, C), f32),
    ((768, C), f32),
    ((8, PAIRS), f32),
    ((64, 128), f32),
    ((16, ATOMS), f32),
    ((6, 8, 128), f32),
    ((8, 8, 128), f32),
)


def solution(mesh):
    sizes = (mesh.shape["gx"], mesh.shape["gy"])

    def per_device(positions, species, face_rows, corner_rows, pair_recv, pair_send, *rest):
        block_count = rest[0]
        params = list(rest[1:])
        params[6] = params[6].reshape(1, -1)
        params[8] = params[8].reshape(1, -1)
        vmem = pl.BlockSpec(memory_space=pltpu.VMEM)
        smem = pl.BlockSpec(memory_space=pltpu.SMEM)
        remote = {"collective_id": 0} if sizes != (1, 1) else {}
        forces, energies = pl.pallas_call(
            partial(kernel_body, sizes),
            out_shape=[
                jax.ShapeDtypeStruct((3, ATOMS), f32),
                jax.ShapeDtypeStruct((1, ATOMS), f32),
            ],
            in_specs=[vmem] * 6 + [smem] + [vmem] * len(params),
            out_specs=[vmem, vmem],
            scratch_shapes=[pltpu.VMEM(s, d) for s, d in SCRATCH]
            + [pltpu.SemaphoreType.DMA((32,)), pltpu.SemaphoreType.DMA((32,))],
            compiler_params=pltpu.CompilerParams(
                has_side_effects=True, vmem_limit_bytes=60 * 1024 * 1024, **remote
            ),
        )(
            positions,
            species.reshape(1, -1),
            face_rows,
            corner_rows,
            pair_recv,
            pair_send,
            block_count,
            *params,
        )
        return forces, energies.reshape(-1)

    return jax.shard_map(
        per_device,
        mesh=mesh,
        in_specs=(
            P(None, ("gx", "gy")),
            P(("gx", "gy")),
            P(None, ("gx", "gy")),
            P(None, ("gx", "gy")),
            P(("gx", "gy"), None),
            P(("gx", "gy"), None),
            P(("gx", "gy")),
        )
        + (P(),) * 9,
        out_specs=(P(None, ("gx", "gy")), P(("gx", "gy"))),
        check_vma=False,
    )
```

time: 2040 us -> 183 us (0.09); the launches traced: 2010 us -> 183 us
  starting transfers between devices: 1220 us -> 0 us
  other arithmetic: 371 us -> 0 us
  local copies, waits for them, and re-layouts: 333 us -> 3.31 us
  Pallas kernels: 0 us -> 178 us
  matrix products: 66.2 us -> 0 us
    ppermute x48 -> x0, starting transfers between devices: 1220 us -> none  [passed_along(): lax.ppermute(array, axis, [(i, (i + by) % size) for i in range(size)])]
    scatter-add x51 -> x0, other arithmetic: 202 us -> none  [the longest x20 96.9 us: backward_add_group(): grad_pos.at[:, senders].add(grad_vectors).at[:, receivers]]
    pallas_call x0 -> x1, Pallas kernels: none -> 178 us  [per_device(): pl.pallas_call(partial(kernel_body, sizes), out_shape=[jax.ShapeDtypeStru...]
    gather x126 -> x0, local copies, waits for them, and re-layouts: 153 us -> none  [the longest x10 29.5 us: backward_add_group(): cotangent = jnp.take(grad_accum, receivers, axis=0).reshape(-1, 9, channels)]
    select_n x108 -> x0, other arithmetic: 67.9 us -> none  [the longest x20 38.9 us: backward_add_group(): cotangent = jnp.take(grad_accum, receivers, axis=0).reshape(-1, 9, channels)]
    dot_general x102 -> x0, matrix products: 66.2 us -> none  [the longest x30 36.2 us: pair_messages(): radial = jnp.dot(hidden_two, radial_out, precision=highest)]
    select_n x30 -> x0, local copies, waits for them, and re-layouts: 56.2 us -> none  [the longest x10 31.2 us: backward_add_group(): cotangent = jnp.take(grad_accum, receivers, axis=0).reshape(-1, 9, channels)]
    reduce_sum x64 -> x0, other arithmetic: 32.6 us -> none  [the longest x10 29.9 us: pair_messages(): expanded * jnp.transpose(harmonic_vals)[:, :, None]]
  transfers between devices with their start and end apart: 48 -> 0, of which waited for: 3 -> 0; matrix products, arithmetic and copies ran while one was open for 2% -> 0% of each run, Pallas kernels for 0% -> 0%
where the time goes in v1:
time: 183 us
  Pallas kernels  178 us (97%)
  local copies, waits for them, and re-layouts  3.31 us (2%)
    pallas_call x1, Pallas kernels, per_device(): pl.pallas_call(partial(kernel_body, sizes), out_shape=[jax.ShapeDtypeStru...  178 us

profile of v1, /device:TPU:1, one launch (start us, length us, event | category | flops | bytes accessed | tf_op | source)
XLA Modules:
  0.0 182.9 jit_solution(382827026799969988)
XLA Ops:
  1.3 1.4 copy.18.readout_hidden
  2.7 178.3 %shard_map.167 = (f32[3,256]{1,0:T(4,128)}, f32[1,256]{1,0:T(1,128)}) custom-call(f32[3,256]{1,0:T(4,128)} %pos.1, s32[1,256]{1,0:T(1,128)} %bitcast.5, s32[4,128]{1,0:T(4,128)} %face_rows.1, s32[4,64]{1,0:T(4,128)} %corner_rows.1, s32[52,128]{1,0:T(8,128)} %pair_recv.1, s32[52,128]{1,0:T(8,128)} %pair_send.1, s32[1]{0:T(128)S(6)} %copy.21.block_count, ...), custom_call_target="tpu_custom_call" | custom-call | tf_op jit(solution)/shard_map/pallas_call | solution.py:647
  181.0 0.0 copy-start
  181.0 0.7 copy-done
  181.7 0.0 copy-start.1
  181.7 0.6 copy.22
  182.3 0.1 copy-done.1
  182.4 0.6 copy.23
Async XLA Ops:
  181.0 0.7 copy-start
  181.7 0.7 copy-start.1

commit v2 on v1

--- a/solution.py
+++ b/solution.py
@@ -20,8 +20,10 @@
 NBLK = 52
 PB = 128
 PAIRS = NBLK * PB
-TM = 512
-T = 256
+TM = 1664
+T = 512
+TILES = PAIRS // T
+TB = 1664
 SUB = 128
 ROWS = 56
 STEPS = ((1, 0), (-1, 0), (0, 1), (0, -1), (1, 1), (1, -1), (-1, 1), (-1, -1))
@@ -119,7 +121,6 @@
         georow,
         sendrow,
         recvm,
-        ohs,
         ohr,
         emb3,
         win4,
@@ -133,14 +134,17 @@
         z2s,
         rs,
         fg,
-        msg,
+        msg_a,
+        msg_b,
         acc,
         acc1,
         acc2,
         gacc,
-        gbuf,
+        gbuf_a,
+        gbuf_b,
         gf,
         gr,
+        gys,
         ge,
         f0t,
         f1t,
@@ -227,14 +231,12 @@
     sent = copies(0, lambda k: posout.at[tile_of(k)], lambda k: posin.at[k], 1)
     start(sent)
 
-    ext_sub = lax.broadcasted_iota(i32, (EXT, PB), 0)
     live = lax.broadcasted_iota(i32, (NBLK, PB), 0) < block_count[0]
     recvm[...] = jnp.where(live, pair_recv[...], -1)
 
     def build(b, carry):
         cols = pl.ds(pl.multiple_of(b * PB, PB), PB)
         send = pair_send[pl.ds(b, 1), :]
-        ohs[:, cols] = (ext_sub == send).astype(bf16)
         ohr[:, cols] = (atom_sub == recvm[pl.ds(b, 1), :]).astype(bf16)
         sendrow[0:1, cols] = send
         return carry
@@ -269,7 +271,7 @@
         bout1[...] = hi
 
     prepare(0)
-    species16 = lax.broadcasted_iota(i32, (128, T), 0) & 15
+    species16 = lax.broadcasted_iota(i32, (128, ATOMS), 0) & 15
     f0t[...] = dot(emb3[...], (species16 == species[...]).astype(bf16))
 
     finish(sent)
@@ -359,20 +361,49 @@
     def radial_all():
         lax.fori_loop(0, PAIRS // TM, radial_pass, 0)
 
-    def first_senders(cols):
-        return dot(emb3[...], (species16 == georow[7:8, cols].astype(i32)).astype(bf16))
-
-    def second_senders(cols):
-        both = dot(fext[...], ohs[:, cols])
-        return both[0:C] + both[C : 2 * C]
-
-    def forward(t, senders):
+    def sender_hot(cols, width):
+        rows = lax.broadcasted_iota(jnp.int16, (EXT, width), 0)
+        return jnp.where(rows == sendrow[0:1, cols].astype(jnp.int16), bf16(1), bf16(0))
+
+    def first_senders():
+        kinds = lax.broadcasted_iota(i32, (128, TM), 0) & 15
+
+        def step(i, carry):
+            cols = pl.ds(pl.multiple_of(i * TM, TM), TM)
+            fg[:, cols] = dot(emb3[...], (kinds == georow[7:8, cols].astype(i32)).astype(bf16))
+            return carry
+
+        lax.fori_loop(0, PAIRS // TM, step, 0)
+
+    def second_senders():
+        def step(i, carry):
+            cols = pl.ds(pl.multiple_of(i * T, T), T)
+            both = dot(fext[...], sender_hot(cols, T))
+            fg[:, cols] = both[0:C] + both[C : 2 * C]
+            return carry
+
+        lax.fori_loop(0, TILES, step, 0)
+
+    def in_pairs(before, beside):
+        before(0, 0)
+
+        def step(j, carry):
+            before(2 * j + 1, 1)
+            beside(2 * j, 0)
+            before(2 * j + 2, 0)
+            beside(2 * j + 1, 1)
+            return carry
+
+        lax.fori_loop(0, TILES // 2, step, 0)
+        beside(TILES - 1, 0)
+
+    def forward(t):
         acc[...] = jnp.zeros_like(acc)
-
-        def step(i, carry):
+        bufs = (msg_a, msg_b)
+
+        def produce(i, which):
+            msg = bufs[which]
             base = pl.multiple_of(i * T, T)
-            cols = pl.ds(base, T)
-            fg[:, cols] = senders(cols)
             for s in range(0, T, SUB):
                 sub = pl.ds(pl.multiple_of(base + s, SUB), SUB)
                 ys = [jnp.broadcast_to(georow[8 + m : 9 + m, sub], (16, SUB)) for m in range(8)]
@@ -384,11 +415,12 @@
                         hi, lo = split2(value)
                         msg[m * C + c : m * C + c + 16, s : s + SUB] = hi
                         msg[m * C + c : m * C + c + 16, T + s : T + s + SUB] = lo
-            hot = ohr[:, cols]
-            acc[...] += dot_nt(msg[...], jnp.concatenate([hot, hot], axis=1))
-            return carry
-
-        lax.fori_loop(0, PAIRS // T, step, 0)
+
+        def consume(i, which):
+            hot = ohr[:, pl.ds(pl.multiple_of(i * T, T), T)]
+            acc[...] += dot_nt(bufs[which][...], jnp.concatenate([hot, hot], axis=1))
+
+        in_pairs(produce, consume)
         sums[t][...] = acc[...] * INV_NEIGH
 
     def invariants(t):
@@ -422,16 +454,19 @@
             gacc[m * C : (m + 1) * C, ATOMS : 2 * ATOMS] = lo
 
     def backward(first):
-        def step(i, carry):
+        bufs = (gbuf_a, gbuf_b)
+
+        def fetch(i, which):
+            hot = ohr[:, pl.ds(pl.multiple_of(i * T, T), T)]
+            bufs[which][...] = dot(gacc[...], jnp.concatenate([hot, hot], axis=0))
+
+        def channels(i, which):
+            gbuf = bufs[which]
             base = pl.multiple_of(i * T, T)
-            cols = pl.ds(base, T)
-            hot = ohr[:, cols]
-            gbuf[...] = dot(gacc[...], jnp.concatenate([hot, hot], axis=0))
-            gys = []
             for s in range(0, T, SUB):
                 sub = pl.ds(pl.multiple_of(base + s, SUB), SUB)
                 ys = [jnp.broadcast_to(georow[8 + m : 9 + m, sub], (16, SUB)) for m in range(8)]
-                dy = [jnp.zeros((16, SUB), f32) for m in range(8)]
+                dy = [jnp.zeros((8, SUB), f32) for m in range(8)]
                 for c in range(0, C, 16):
                     f = fg[c : c + 16, sub]
                     r = [rs[l * C + c : l * C + c + 16, sub] for l in range(3)]
@@ -443,22 +478,33 @@
                         term = g if m == 0 else g * ys[m - 1]
                         tot[l] = term if tot[l] is None else tot[l] + term
                         if m > 0:
-                            dy[m - 1] = dy[m - 1] + p[l] * g
+                            part = p[l] * g
+                            dy[m - 1] = dy[m - 1] + (part[0:8] + part[8:16])
                     if not first:
-                        gfv = r[0] * tot[0] + r[1] * tot[1] + r[2] * tot[2]
-                        hi, lo = split2(gfv)
-                        gf[c : c + 16, s : s + SUB] = hi
-                        gf[C + c : C + c + 16, s : s + SUB] = lo
+                        hi, lo = split2(r[0] * tot[0] + r[1] * tot[1] + r[2] * tot[2])
+                        gf[c : c + 16, sub] = hi
+                        gf[C + c : C + c + 16, sub] = lo
                     for l in range(3):
-                        hi, lo = split2(tot[l] * f)
-                        gr[l * C + c : l * C + c + 16, s : s + SUB] = hi
-                        gr[l * C + c : l * C + c + 16, T + s : T + s + SUB] = lo
-                gys.append([jnp.sum(x, axis=0, keepdims=True) for x in dy])
-            gy = [jnp.concatenate([part[m] for part in gys], axis=1) for m in range(8)]
-            if not first:
-                ge[...] += dot_nt(ohs[:, cols], gf[...])
-            both = dot(bout2[...], gr[:, 0:T])
-            gh2 = both[0:RH] + both[RH : 2 * RH] + dot(bout1[...], gr[:, T : 2 * T])
+                        gr[l * C + c : l * C + c + 16, sub] = tot[l] * f
+                for m in range(8):
+                    gys[m : m + 1, sub] = jnp.sum(dy[m], axis=0, keepdims=True)
+
+        in_pairs(fetch, channels)
+
+        if not first:
+
+            def scatter(i, carry):
+                cols = pl.ds(pl.multiple_of(i * T, T), T)
+                ge[...] += dot_nt(sender_hot(cols, T), gf[:, cols])
+                return carry
+
+            lax.fori_loop(0, TILES, scatter, 0)
+
+        def radial_back(i, carry):
+            cols = pl.ds(pl.multiple_of(i * TB, TB), TB)
+            hi, lo = split2(gr[:, cols])
+            both = dot(bout2[...], hi)
+            gh2 = both[0:RH] + both[RH : 2 * RH] + dot(bout1[...], lo)
             z2 = z2s[:, cols]
             sg = jax.nn.sigmoid(z2)
             gh1 = dot(bmid4[...], activations(gh2 * (sg * (1.0 + z2 * (1.0 - sg)))))
@@ -466,7 +512,8 @@
             sg = jax.nn.sigmoid(z1)
             gb = dot(bin4[...], activations(gh1 * (sg * (1.0 + z1 * (1.0 - sg)))))[0:NB]
             geo = georow[:, cols]
-            away, bump = basis_of(geo, T)
+            gy = [gys[m : m + 1, cols] for m in range(8)]
+            away, bump = basis_of(geo, TB)
             slope = bump * (geo[6:7] - (2.0 * SHARP) * away * geo[5:6])
             gdist = jnp.sum(gb * slope, axis=0, keepdims=True)
             ux, uy, uz = geo[1:2], geo[2:3], geo[3:4]
@@ -483,23 +530,24 @@
             else:
                 out = [out[n] + gv[n : n + 1, cols] for n in range(3)]
                 cut = [parts2(x) for x in out]
-                zero = jnp.zeros((2, T), f32)
+                zero = jnp.zeros((2, TB), f32)
                 base8 = jnp.concatenate([x[0] for x in cut] + [x[1] for x in cut] + [zero], axis=0)
                 idx = sendrow[0:1, cols]
                 high = lax.shift_right_logical(idx, 7)
                 lhs = jnp.concatenate(
                     [jnp.where(high == h, base8, 0.0) for h in range(8)], axis=0
                 ).astype(bf16)
-                low = (lax.broadcasted_iota(i32, (128, T), 0) == (idx & 127)).astype(bf16)
+                low = (lax.broadcasted_iota(i32, (128, TB), 0) == (idx & 127)).astype(bf16)
                 fs[...] += dot_nt(lhs, low)
-                lhs = jnp.concatenate([base8, jnp.zeros((8, T), f32)], axis=0).astype(bf16)
-                fr[...] += dot_nt(lhs, hot)
+                lhs = jnp.concatenate([base8, jnp.zeros((8, TB), f32)], axis=0).astype(bf16)
+                fr[...] += dot_nt(lhs, ohr[:, cols])
             return carry
 
-        lax.fori_loop(0, PAIRS // T, step, 0)
+        lax.fori_loop(0, PAIRS // TB, radial_back, 0)
 
     radial_all()
-    forward(0, first_senders)
+    first_senders()
+    forward(0)
     f1t[...] = node(0, f0t[...])
 
     feat = f1t[...]
@@ -510,7 +558,6 @@
         1, lambda k: fsend.at[pl.ds(*slot_of(k))], lambda k: fghost.at[pl.ds(*slot_of(k))], 1
     )
     start(sent)
-    gsend[0:ATOMS, :] = jnp.zeros((ATOMS, C), f32)
     prepare(1)
     prepare_back(1)
     radial_all()
@@ -522,7 +569,8 @@
     fext[0:C, ATOMS:EXT] = hi
     fext[C : 2 * C, ATOMS:EXT] = lo
 
-    forward(1, second_senders)
+    second_senders()
+    forward(1)
     second = node(1, feat)
     hidden = dot_exact(readout_hidden[...].T, second)
     sg = jax.nn.sigmoid(hidden)
@@ -549,12 +597,7 @@
     prepare_back(0)
     radial_all()
 
-    def senders_pass(i, carry):
-        cols = pl.ds(pl.multiple_of(i * T, T), T)
-        fg[:, cols] = first_senders(cols)
-        return carry
-
-    lax.fori_loop(0, PAIRS // T, senders_pass, 0)
+    first_senders()
     fs[...] = jnp.zeros_like(fs)
     fr[...] = jnp.zeros_like(fr)
     finish(sent)
@@ -594,7 +637,6 @@
     ((16, PAIRS), f32),
     ((8, PAIRS), i32),
     ((NBLK, PB), i32),
-    ((EXT, PAIRS), bf16),
     ((ATOMS, PAIRS), bf16),
     ((C, 128), bf16),
     ((RH, 4 * NB), bf16),
@@ -609,13 +651,16 @@
     ((3 * C, PAIRS), f32),
     ((C, PAIRS), f32),
     ((9 * C, 2 * T), bf16),
+    ((9 * C, 2 * T), bf16),
     ((9 * C, ATOMS), f32),
     ((9 * C, ATOMS), f32),
     ((9 * C, ATOMS), f32),
     ((9 * C, 2 * ATOMS), bf16),
     ((9 * C, T), f32),
-    ((2 * C, T), bf16),
-    ((3 * C, 2 * T), bf16),
+    ((9 * C, T), f32),
+    ((2 * C, PAIRS), bf16),
+    ((3 * C, PAIRS), f32),
+    ((8, PAIRS), f32),
     ((EXT, 2 * C), f32),
     ((C, ATOMS), f32),
     ((C, ATOMS), f32),

time: 183 us -> 129 us (0.70)
  Pallas kernels: 178 us -> 124 us
    pallas_call x1, Pallas kernels: 178 us -> 124 us  [per_device(): pl.pallas_call(partial(kernel_body, sizes), out_shape=[jax.ShapeDtypeStru...]
where the time goes in v2:
time: 129 us; the launch traced here: 128 us
  Pallas kernels  124 us (96%)
  local copies, waits for them, and re-layouts  3.31 us (3%)
  between operations  1.3 us (1%)
    pallas_call x1, Pallas kernels, per_device(): pl.pallas_call(partial(kernel_body, sizes), out_shape=[jax.ShapeDtypeStru...  124 us
    unnamed x7, local copies, waits for them, and re-layouts  3.31 us

profile of v2, /device:TPU:1, one launch (start us, length us, event | category | flops | bytes accessed | tf_op | source)
XLA Modules:
  0.0 128.2 jit_solution(17572650406797136428)
XLA Ops:
  1.3 1.4 %copy.18.readout_hidden = f32[128,16]{1,0:T(8,128)} copy(f32[128,16]{0,1:T(8,128)} %param.30) | data formatting | bytes 16384 | tf_op args[14]
  2.7 123.6 %shard_map.167 = (f32[3,256]{1,0:T(4,128)}, f32[1,256]{1,0:T(1,128)}) custom-call(f32[3,256]{1,0:T(4,128)} %pos.1, s32[1,256]{1,0:T(1,128)} %bitcast.5, s32[4,128]{1,0:T(4,128)} %face_rows.1, s32[4,64]{1,0:T(4,128)} %corner_rows.1, s32[52,128]{1,0:T(8,128)} %pair_recv.1, s32[52,128]{1,0:T(8,128)} %pair_send.1, s32[1]{0:T(128)S(6)} %copy.21.block_count, ...), custom_call_target="tpu_custom_call" | custom-call | tf_op jit(solution)/shard_map/pallas_call | solution.py:692
  126.3 0.0 copy-start
  126.3 0.7 copy-done
  127.0 0.0 copy-start.1
  127.0 0.6 copy.22
  127.6 0.1 copy-done.1
  127.7 0.6 copy.23
Async XLA Ops:
  126.3 0.7 copy-start
  127.0 0.7 copy-start.1

commit v3 on v2

--- a/solution.py
+++ b/solution.py
@@ -136,7 +136,6 @@
         fg,
         msg_a,
         msg_b,
-        acc,
         acc1,
         acc2,
         gacc,
@@ -157,6 +156,10 @@
         gv,
         fs,
         fr,
+        gback,
+        gvp,
+        hot_a,
+        hot_b,
         gpout,
         gpin,
         send_sem,
@@ -375,15 +378,6 @@
 
         lax.fori_loop(0, PAIRS // TM, step, 0)
 
-    def second_senders():
-        def step(i, carry):
-            cols = pl.ds(pl.multiple_of(i * T, T), T)
-            both = dot(fext[...], sender_hot(cols, T))
-            fg[:, cols] = both[0:C] + both[C : 2 * C]
-            return carry
-
-        lax.fori_loop(0, TILES, step, 0)
-
     def in_pairs(before, beside):
         before(0, 0)
 
@@ -397,7 +391,21 @@
         lax.fori_loop(0, TILES // 2, step, 0)
         beside(TILES - 1, 0)
 
+    hots = (hot_a, hot_b)
+
+    def build_hot(i, which):
+        hots[which][...] = sender_hot(pl.ds(pl.multiple_of(i * T, T), T), T)
+
+    def second_senders():
+        def step(i, which):
+            cols = pl.ds(pl.multiple_of(i * T, T), T)
+            both = dot(fext[...], hots[which][...])
+            fg[:, cols] = both[0:C] + both[C : 2 * C]
+
+        in_pairs(build_hot, step)
+
     def forward(t):
+        acc = sums[t]
         acc[...] = jnp.zeros_like(acc)
         bufs = (msg_a, msg_b)
 
@@ -421,7 +429,7 @@
             acc[...] += dot_nt(bufs[which][...], jnp.concatenate([hot, hot], axis=1))
 
         in_pairs(produce, consume)
-        sums[t][...] = acc[...] * INV_NEIGH
+        acc[...] = acc[...] * INV_NEIGH
 
     def invariants(t):
         accn = sums[t]
@@ -491,15 +499,15 @@
 
         in_pairs(fetch, channels)
 
-        if not first:
-
-            def scatter(i, carry):
-                cols = pl.ds(pl.multiple_of(i * T, T), T)
-                ge[...] += dot_nt(sender_hot(cols, T), gf[:, cols])
-                return carry
-
-            lax.fori_loop(0, TILES, scatter, 0)
-
+    def scatter_features():
+        def step(i, which):
+            cols = pl.ds(pl.multiple_of(i * T, T), T)
+            ge[...] += dot_nt(hots[which][...], gf[:, cols])
+
+        ge[...] = jnp.zeros_like(ge)
+        in_pairs(build_hot, step)
+
+    def backward_radial():
         def radial_back(i, carry):
             cols = pl.ds(pl.multiple_of(i * TB, TB), TB)
             hi, lo = split2(gr[:, cols])
@@ -512,40 +520,45 @@
             sg = jax.nn.sigmoid(z1)
             gb = dot(bin4[...], activations(gh1 * (sg * (1.0 + z1 * (1.0 - sg)))))[0:NB]
             geo = georow[:, cols]
-            gy = [gys[m : m + 1, cols] for m in range(8)]
             away, bump = basis_of(geo, TB)
             slope = bump * (geo[6:7] - (2.0 * SHARP) * away * geo[5:6])
-            gdist = jnp.sum(gb * slope, axis=0, keepdims=True)
-            ux, uy, uz = geo[1:2], geo[2:3], geo[3:4]
-            gux = Q3 * gy[0] + Q15 * (uy * gy[3] + uz * gy[6] + ux * gy[7])
-            guy = Q3 * gy[1] + Q15 * (ux * gy[3] + uz * gy[4] - uy * gy[7])
-            guz = Q3 * gy[2] + Q15 * (uy * gy[4] + ux * gy[6]) + (3.0 * Q5) * uz * gy[5]
-            along = gux * ux + guy * uy + guz * uz
-            inv = geo[4:5]
-            pull = gdist - inv * along
-            out = [pull * ux + inv * gux, pull * uy + inv * guy, pull * uz + inv * guz]
-            if not first:
-                for n in range(3):
-                    gv[n : n + 1, cols] = out[n]
-            else:
-                out = [out[n] + gv[n : n + 1, cols] for n in range(3)]
-                cut = [parts2(x) for x in out]
-                zero = jnp.zeros((2, TB), f32)
-                base8 = jnp.concatenate([x[0] for x in cut] + [x[1] for x in cut] + [zero], axis=0)
-                idx = sendrow[0:1, cols]
-                high = lax.shift_right_logical(idx, 7)
-                lhs = jnp.concatenate(
-                    [jnp.where(high == h, base8, 0.0) for h in range(8)], axis=0
-                ).astype(bf16)
-                low = (lax.broadcasted_iota(i32, (128, TB), 0) == (idx & 127)).astype(bf16)
-                fs[...] += dot_nt(lhs, low)
-                lhs = jnp.concatenate([base8, jnp.zeros((8, TB), f32)], axis=0).astype(bf16)
-                fr[...] += dot_nt(lhs, ohr[:, cols])
+            gys[8:9, cols] = jnp.sum(gb * slope, axis=0, keepdims=True)
             return carry
 
         lax.fori_loop(0, PAIRS // TB, radial_back, 0)
 
+    def backward_geometry():
+        for b in range(NBLK):
+            gback[pl.ds(b, 16, stride=ROWS), :] = gys[:, b * PB : (b + 1) * PB]
+        gy = [gback[m * ROWS : m * ROWS + NBLK, :] for m in range(9)]
+        ux, uy, uz, inv = [geop[n * ROWS : n * ROWS + NBLK, :] for n in range(1, 5)]
+        gux = Q3 * gy[0] + Q15 * (uy * gy[3] + uz * gy[6] + ux * gy[7])
+        guy = Q3 * gy[1] + Q15 * (ux * gy[3] + uz * gy[4] - uy * gy[7])
+        guz = Q3 * gy[2] + Q15 * (uy * gy[4] + ux * gy[6]) + (3.0 * Q5) * uz * gy[5]
+        along = gux * ux + guy * uy + guz * uz
+        pull = gy[8] - inv * along
+        return [pull * ux + inv * gux, pull * uy + inv * guy, pull * uz + inv * guz]
+
+    def scatter_positions():
+        def step(i, carry):
+            cols = pl.ds(pl.multiple_of(i * TB, TB), TB)
+            base8 = gv[:, cols]
+            idx = sendrow[0:1, cols]
+            high = lax.shift_right_logical(idx, 7)
+            parts = jnp.concatenate(
+                [jnp.where(high == h, base8, 0.0) for h in range(8)], axis=0
+            ).astype(bf16)
+            rows = lax.broadcasted_iota(jnp.int16, (128, TB), 0)
+            low = jnp.where(rows == (idx & 127).astype(jnp.int16), bf16(1), bf16(0))
+            fs[...] += dot_nt(low, parts)
+            whole = jnp.concatenate([base8, jnp.zeros((8, TB), f32)], axis=0).astype(bf16)
+            fr[...] += dot_nt(ohr[:, cols], whole)
+            return carry
+
+        lax.fori_loop(0, PAIRS // TB, step, 0)
+
     radial_all()
+    gys[8:16, :] = jnp.zeros((8, PAIRS), f32)
     first_senders()
     forward(0)
     f1t[...] = node(0, f0t[...])
@@ -582,8 +595,8 @@
     gsecond = dot_exact(readout_hidden[...], ghidden)
     gfirst[...] = readout_linear[...].T + dot_exact(self_weight[1], gsecond)
     node_back(1, gsecond)
-    ge[...] = jnp.zeros_like(ge)
     backward(False)
+    scatter_features()
 
     gsend[...] = ge[:, 0:C] + ge[:, C : 2 * C]
 
@@ -593,6 +606,11 @@
 
     sent = copies(2, ghost, lambda k: gret.at[pl.ds(*slot_of(k))], -1)
     start(sent)
+    backward_radial()
+    out = backward_geometry()
+    gvp[...] = jnp.zeros_like(gvp)
+    for n in range(3):
+        gvp[n * ROWS : n * ROWS + NBLK, :] = out[n]
     prepare(0)
     prepare_back(0)
     radial_all()
@@ -605,17 +623,28 @@
     mine = gsend[0:ATOMS, :] + returned[:, 0:C] + returned[:, C : 2 * C] + returned[:, 2 * C :]
     node_back(0, gfirst[...] + mine.T)
     backward(True)
+    backward_radial()
+    out = backward_geometry()
+    for n in range(3):
+        hi, lo = parts2(out[n] + gvp[n * ROWS : n * ROWS + NBLK, :])
+        gvp[n * ROWS : n * ROWS + NBLK, :] = hi
+        gvp[(n + 3) * ROWS : (n + 3) * ROWS + NBLK, :] = lo
+    for b in range(NBLK):
+        gv[:, b * PB : (b + 1) * PB] = gvp[pl.ds(b, 8, stride=ROWS), :]
+    scatter_positions()
 
     nothing = jnp.zeros((5, 128), f32)
+    by_atom = fs[...].T
+    by_receiver = fr[...].T
     tiles = []
     for h in range(8):
-        part = fs[8 * h : 8 * h + 8, :]
+        part = by_atom[8 * h : 8 * h + 8, :]
         tiles.append(jnp.concatenate([part[0:3] + part[3:6], nothing], axis=0))
     for h in range(6):
         gpout[h] = tiles[h + 2]
     sent = copies(3, lambda k: gpout.at[tile_of(k)], lambda k: gpin.at[k], -1)
     start(sent)
-    own = jnp.concatenate(tiles[0:2], axis=1)[0:3] - (fr[0:3, :] + fr[3:6, :])
+    own = jnp.concatenate(tiles[0:2], axis=1)[0:3] - (by_receiver[0:3] + by_receiver[3:6])
     finish(sent)
     back = [gpin[k] for k in range(4)]
     back.append(jnp.where(low_half, gpin[4], gpin[5]))
@@ -654,13 +683,12 @@
     ((9 * C, 2 * T), bf16),
     ((9 * C, ATOMS), f32),
     ((9 * C, ATOMS), f32),
-    ((9 * C, ATOMS), f32),
     ((9 * C, 2 * ATOMS), bf16),
     ((9 * C, T), f32),
     ((9 * C, T), f32),
     ((2 * C, PAIRS), bf16),
     ((3 * C, PAIRS), f32),
-    ((8, PAIRS), f32),
+    ((16, PAIRS), f32),
     ((EXT, 2 * C), f32),
     ((C, ATOMS), f32),
     ((C, ATOMS), f32),
@@ -671,8 +699,12 @@
     ((EXT, C), f32),
     ((768, C), f32),
     ((8, PAIRS), f32),
-    ((64, 128), f32),
-    ((16, ATOMS), f32),
+    ((128, 64), f32),
+    ((ATOMS, 16), f32),
+    ((16 * ROWS, 128), f32),
+    ((8 * ROWS, 128), f32),
+    ((EXT, T), bf16),
+    ((EXT, T), bf16),
     ((6, 8, 128), f32),
     ((8, 8, 128), f32),
 )
@@ -700,7 +732,7 @@
             scratch_shapes=[pltpu.VMEM(s, d) for s, d in SCRATCH]
             + [pltpu.SemaphoreType.DMA((32,)), pltpu.SemaphoreType.DMA((32,))],
             compiler_params=pltpu.CompilerParams(
-                has_side_effects=True, vmem_limit_bytes=60 * 1024 * 1024, **remote
+                has_side_effects=True, vmem_limit_bytes=62 * 1024 * 1024, **remote
             ),
         )(
             positions,

time: 129 us -> 125 us (0.969)
  Pallas kernels: 124 us -> 121 us
    pallas_call x1, Pallas kernels: 124 us -> 121 us  [per_device(): pl.pallas_call(partial(kernel_body, sizes), out_shape=[jax.ShapeDtypeStru...]
where the time goes in v3:
time: 125 us
  Pallas kernels  121 us (97%)
  local copies, waits for them, and re-layouts  3.31 us (3%)
  between operations  1.3 us (1%)
    pallas_call x1, Pallas kernels, per_device(): pl.pallas_call(partial(kernel_body, sizes), out_shape=[jax.ShapeDtypeStru...  121 us
    unnamed x7, local copies, waits for them, and re-layouts  3.31 us

profile of v3, /device:TPU:1, one launch (start us, length us, event | category | flops | bytes accessed | tf_op | source)
XLA Modules:
  0.0 125.2 jit_solution(6664984395827853263)
XLA Ops:
  1.3 1.4 %copy.18.readout_hidden = f32[128,16]{1,0:T(8,128)} copy(f32[128,16]{0,1:T(8,128)} %param.30) | data formatting | bytes 16384 | tf_op args[14]
  2.7 120.6 %shard_map.167 = (f32[3,256]{1,0:T(4,128)}, f32[1,256]{1,0:T(1,128)}) custom-call(f32[3,256]{1,0:T(4,128)} %pos.1, s32[1,256]{1,0:T(1,128)} %bitcast.5, s32[4,128]{1,0:T(4,128)} %face_rows.1, s32[4,64]{1,0:T(4,128)} %corner_rows.1, s32[52,128]{1,0:T(8,128)} %pair_recv.1, s32[52,128]{1,0:T(8,128)} %pair_send.1, s32[1]{0:T(128)S(6)} %copy.21.block_count, ...), custom_call_target="tpu_custom_call" | custom-call | tf_op jit(solution)/shard_map/pallas_call | solution.py:724
  123.3 0.0 copy-start
  123.3 0.7 copy-done
  124.0 0.0 copy-start.1
  124.0 0.6 copy.22
  124.6 0.1 copy-done.1
  124.7 0.6 copy.23
Async XLA Ops:
  123.3 0.7 copy-start
  124.0 0.7 copy-start.1

commit v4 on v3

--- a/solution.py
+++ b/solution.py
@@ -33,7 +33,7 @@
 Q5 = 5.0**0.5
 Q15 = 15.0**0.5
 INV_NEIGH = 0.25
-HIGH = lax.Precision.HIGHEST
+HIGH = lax.Precision.HIGH
 MESH = pl.DeviceIdType.MESH
 L_OF_M = (0, 1, 1, 1, 2, 2, 2, 2, 2)
 
@@ -217,8 +217,6 @@
     atom_lane = lax.broadcasted_iota(i32, (128, ATOMS), 1)
     for h in range(6):
         oh6[:, h * 128 : (h + 1) * 128] = (atom_sub == rows6[h : h + 1, :]).astype(bf16)
-        col = jnp.broadcast_to(rows_t[:, h : h + 1], (128, ATOMS)).astype(i32)
-        oh6t[h * 128 : (h + 1) * 128, :] = (atom_lane == col).astype(bf16)
 
     psrc[...] = jnp.zeros_like(psrc)
     psrc[0:3, :] = pos[...]
@@ -236,6 +234,9 @@
 
     live = lax.broadcasted_iota(i32, (NBLK, PB), 0) < block_count[0]
     recvm[...] = jnp.where(live, pair_recv[...], -1)
+    for h in range(6):
+        col = jnp.broadcast_to(rows_t[:, h : h + 1], (128, ATOMS)).astype(i32)
+        oh6t[h * 128 : (h + 1) * 128, :] = (atom_lane == col).astype(bf16)
 
     def build(b, carry):
         cols = pl.ds(pl.multiple_of(b * PB, PB), PB)
@@ -364,8 +365,8 @@
     def radial_all():
         lax.fori_loop(0, PAIRS // TM, radial_pass, 0)
 
-    def sender_hot(cols, width):
-        rows = lax.broadcasted_iota(jnp.int16, (EXT, width), 0)
+    def sender_hot(cols, width, first, count):
+        rows = lax.broadcasted_iota(jnp.int16, (count, width), 0) + jnp.int16(first)
         return jnp.where(rows == sendrow[0:1, cols].astype(jnp.int16), bf16(1), bf16(0))
 
     def first_senders():
@@ -379,28 +380,37 @@
         lax.fori_loop(0, PAIRS // TM, step, 0)
 
     def in_pairs(before, beside):
-        before(0, 0)
+        def both(later, at_later, now, at_now):
+            for q in range(4):
+                before(later, at_later, q)
+                beside(now, at_now, q)
+
+        for q in range(4):
+            before(0, 0, q)
 
         def step(j, carry):
-            before(2 * j + 1, 1)
-            beside(2 * j, 0)
-            before(2 * j + 2, 0)
-            beside(2 * j + 1, 1)
+            both(2 * j + 1, 1, 2 * j, 0)
+            both(2 * j + 2, 0, 2 * j + 1, 1)
             return carry
 
         lax.fori_loop(0, TILES // 2, step, 0)
-        beside(TILES - 1, 0)
+        for q in range(4):
+            beside(TILES - 1, 0, q)
 
     hots = (hot_a, hot_b)
 
-    def build_hot(i, which):
-        hots[which][...] = sender_hot(pl.ds(pl.multiple_of(i * T, T), T), T)
+    def build_hot(i, which, q):
+        count = EXT // 4
+        cols = pl.ds(pl.multiple_of(i * T, T), T)
+        hots[which][q * count : (q + 1) * count, :] = sender_hot(cols, T, q * count, count)
 
     def second_senders():
-        def step(i, which):
-            cols = pl.ds(pl.multiple_of(i * T, T), T)
-            both = dot(fext[...], hots[which][...])
-            fg[:, cols] = both[0:C] + both[C : 2 * C]
+        def step(i, which, q):
+            if q % 2 == 0:
+                half = (q // 2) * (T // 2)
+                cols = pl.ds(pl.multiple_of(i * T + half, T // 2), T // 2)
+                both = dot(fext[...], hots[which][:, half : half + T // 2])
+                fg[:, cols] = both[0:C] + both[C : 2 * C]
 
         in_pairs(build_hot, step)
 
@@ -409,10 +419,10 @@
         acc[...] = jnp.zeros_like(acc)
         bufs = (msg_a, msg_b)
 
-        def produce(i, which):
+        def produce(i, which, q):
             msg = bufs[which]
             base = pl.multiple_of(i * T, T)
-            for s in range(0, T, SUB):
+            for s in (q * SUB,):
                 sub = pl.ds(pl.multiple_of(base + s, SUB), SUB)
                 ys = [jnp.broadcast_to(georow[8 + m : 9 + m, sub], (16, SUB)) for m in range(8)]
                 for c in range(0, C, 16):
@@ -424,9 +434,11 @@
                         msg[m * C + c : m * C + c + 16, s : s + SUB] = hi
                         msg[m * C + c : m * C + c + 16, T + s : T + s + SUB] = lo
 
-        def consume(i, which):
-            hot = ohr[:, pl.ds(pl.multiple_of(i * T, T), T)]
-            acc[...] += dot_nt(bufs[which][...], jnp.concatenate([hot, hot], axis=1))
+        def consume(i, which, q):
+            if q % 2 == 0:
+                rows = pl.ds((q // 2) * (9 * C // 2), 9 * C // 2)
+                hot = ohr[:, pl.ds(pl.multiple_of(i * T, T), T)]
+                acc[rows, :] += dot_nt(bufs[which][rows, :], jnp.concatenate([hot, hot], axis=1))
 
         in_pairs(produce, consume)
         acc[...] = acc[...] * INV_NEIGH
@@ -464,14 +476,18 @@
     def backward(first):
         bufs = (gbuf_a, gbuf_b)
 
-        def fetch(i, which):
-            hot = ohr[:, pl.ds(pl.multiple_of(i * T, T), T)]
-            bufs[which][...] = dot(gacc[...], jnp.concatenate([hot, hot], axis=0))
-
-        def channels(i, which):
+        def fetch(i, which, q):
+            if q % 2 == 0:
+                half = (q // 2) * (T // 2)
+                hot = ohr[:, pl.ds(pl.multiple_of(i * T + half, T // 2), T // 2)]
+                bufs[which][:, half : half + T // 2] = dot(
+                    gacc[...], jnp.concatenate([hot, hot], axis=0)
+                )
+
+        def channels(i, which, q):
             gbuf = bufs[which]
             base = pl.multiple_of(i * T, T)
-            for s in range(0, T, SUB):
+            for s in (q * SUB,):
                 sub = pl.ds(pl.multiple_of(base + s, SUB), SUB)
                 ys = [jnp.broadcast_to(georow[8 + m : 9 + m, sub], (16, SUB)) for m in range(8)]
                 dy = [jnp.zeros((8, SUB), f32) for m in range(8)]
@@ -500,9 +516,11 @@
         in_pairs(fetch, channels)
 
     def scatter_features():
-        def step(i, which):
-            cols = pl.ds(pl.multiple_of(i * T, T), T)
-            ge[...] += dot_nt(hots[which][...], gf[:, cols])
+        def step(i, which, q):
+            if q % 2 == 0:
+                rows = pl.ds((q // 2) * (EXT // 2), EXT // 2)
+                cols = pl.ds(pl.multiple_of(i * T, T), T)
+                ge[rows, :] += dot_nt(hots[which][rows, :], gf[:, cols])
 
         ge[...] = jnp.zeros_like(ge)
         in_pairs(build_hot, step)

time: 125 us -> 120 us (0.960)
  Pallas kernels: 121 us -> 115 us
    pallas_call x1, Pallas kernels: 121 us -> 115 us  [per_device(): pl.pallas_call(partial(kernel_body, sizes), out_shape=[jax.ShapeDtypeStru...]
where the time goes in v4:
time: 120 us
  Pallas kernels  115 us (96%)
  local copies, waits for them, and re-layouts  3.31 us (3%)
  between operations  1.3 us (1%)
    pallas_call x1, Pallas kernels, per_device(): pl.pallas_call(partial(kernel_body, sizes), out_shape=[jax.ShapeDtypeStru...  115 us
    unnamed x7, local copies, waits for them, and re-layouts  3.31 us

profile of v4, /device:TPU:1, one launch (start us, length us, event | category | flops | bytes accessed | tf_op | source)
XLA Modules:
  0.0 119.7 jit_solution(12507258908054867538)
XLA Ops:
  1.3 1.4 %copy.18.readout_hidden = f32[128,16]{1,0:T(8,128)} copy(f32[128,16]{0,1:T(8,128)} %param.30) | data formatting | bytes 16384 | tf_op args[14]
  2.7 115.1 %shard_map.167 = (f32[3,256]{1,0:T(4,128)}, f32[1,256]{1,0:T(1,128)}) custom-call(f32[3,256]{1,0:T(4,128)} %pos.1, s32[1,256]{1,0:T(1,128)} %bitcast.5, s32[4,128]{1,0:T(4,128)} %face_rows.1, s32[4,64]{1,0:T(4,128)} %corner_rows.1, s32[52,128]{1,0:T(8,128)} %pair_recv.1, s32[52,128]{1,0:T(8,128)} %pair_send.1, s32[1]{0:T(128)S(6)} %copy.21.block_count, ...), custom_call_target="tpu_custom_call" | custom-call | tf_op jit(solution)/shard_map/pallas_call | solution.py:742
  117.8 0.0 copy-start
  117.8 0.7 copy-done
  118.5 0.0 copy-start.1
  118.5 0.6 copy.22
  119.1 0.1 copy-done.1
  119.2 0.6 copy.23
Async XLA Ops:
  117.8 0.7 copy-start
  118.5 0.7 copy-start.1
